TPU v7x, 32 devices: a whole 2x2x4 slice. The times are simulated.
32 devices in a mesh: member: 4 (over y, x), space: 8 (over z, core).
Axes of the slice: x: 2, y: 2, z: 4, core: 2. Of those that a mesh axis runs over, the one named last changes fastest.
Arguments:
- grid_in: bfloat16 [4, 8192, 256], P('member', 'space'), may hold values from -6 to 6
- mesh_embed: bfloat16 [2048, 512], P('space'), may hold values from -6 to 6
- g2m_src: int32 [8, 8, 256], P('space'), may hold values from 0 to 1023
- g2m_dst: int32 [8, 8, 256], P('space'), may hold values from 0 to 255
- g2m_own_src: int32 [8, 1536], P('space'), may hold values from 0 to 1023
- g2m_own_dst: int32 [8, 1536], P('space'), may hold values from 0 to 255
- g2m_len: int32 [8, 8], P(None, 'space'), may hold values from 0 to 1536, as said below
- mesh_nbr: int32 [2048, 32], P('space'), may hold values from 0 to 383
- halo_rows: int32 [8, 16], P('space'), may hold values from 0 to 255
- m2g_src: int32 [8, 8, 256], P('space'), may hold values from 0 to 255
- m2g_dst: int32 [8, 8, 256], P('space'), may hold values from 0 to 1023
- m2g_own_src: int32 [8, 2560], P('space'), may hold values from 0 to 255
- m2g_own_dst: int32 [8, 2560], P('space'), may hold values from 0 to 1023
- m2g_len: int32 [8, 8], P(None, 'space'), may hold values from 0 to 2560, as said below
- w_embed: bfloat16 [256, 512], replicated, may hold values from -0.375 to 0.375
- w_send: bfloat16 [512, 512], replicated, may hold values from -0.25 to 0.25
- w_mesh: bfloat16 [512, 512], replicated, may hold values from -0.25 to 0.25
- attn_gain: float32 [512], replicated, may hold values from 0.1 to 1.9
- w_query: bfloat16 [512, 512], P('member')
- w_key: bfloat16 [512, 512], P('member')
- w_value: bfloat16 [512, 512], P('member'), may hold values from -0.25 to 0.25
- w_project: bfloat16 [512, 512], P('member'), may hold values from -0.25 to 0.25
- mlp_gain: float32 [512], replicated, may hold values from 0.1 to 1.9
- w_up: bfloat16 [512, 2048], P('member'), may hold values from -0.25 to 0.25
- w_down: bfloat16 [2048, 512], P('member'), may hold values from -0.125 to 0.125
- w_return: bfloat16 [512, 512], replicated, may hold values from -0.25 to 0.25
- w_grid: bfloat16 [512, 512], replicated, may hold values from -0.25 to 0.25
- w_skip: bfloat16 [512, 512], replicated, may hold values from -0.25 to 0.25
- w_out: bfloat16 [512, 84], replicated, may hold values from -0.25 to 0.25
Outputs:
- denoised: bfloat16 [4, 84, 8192], P('member', None, 'space')
Inputs may be any that keep to these rules, and one draw needn't show every extreme that they name: Pairs with |s - d| > 1 are empty (length 0). For |s - d| = 1 slot j carries an edge exactly when j < g2m_len[s, d] <= 256; on the diagonal, slot j of g2m_own_src and g2m_own_dst carries an edge exactly when j < g2m_len[p, p] <= 1536. Other slots hold arbitrary indices. The bands at the two ends of the axis (1 at each) receive the most edges. Pairs with |s - d| > 1 are empty (length 0). For |s - d| = 1 slot j carries an edge exactly when j < m2g_len[s, d] <= 256; on the diagonal, slot j of m2g_own_src and m2g_own_dst carries an edge exactly when j < m2g_len[p, p] <= 2560. Other slots hold arbitrary indices. The bands at the two ends of the axis (1 at each) receive the most edges.
All inputs are finite; a program needn't handle non-finite values.
Results may differ from a plain program's by a relative error of at most 0.015.
Values may be sent and summed in bfloat16 or wider, within the bound.
A program may use at most 64 MiB of HBM per device.

v0:
```python
import math

import jax
import jax.numpy as jnp
from jax import lax
from jax.sharding import PartitionSpec as P

DH = 128


EPS = 1e-05


def from_behind(block, axis, distance):
    devices = range(lax.axis_size(axis))
    route = [(i - distance, i) for i in devices if i - distance in devices]
    return lax.ppermute(block, axis, route)


def layer_norm(values, norm_gain):
    centred = values - jnp.mean(values, axis=-1, keepdims=True)
    spread = jnp.mean(centred * centred, axis=-1, keepdims=True)
    return centred * lax.rsqrt(spread + EPS) * norm_gain


def pick_rows(table, wanted):
    picker = (wanted[:, None] == lax.broadcasted_iota(jnp.int32, (1, table.shape[0]), 1)).astype(
        table.dtype
    )
    return jnp.dot(picker, table, preferred_element_type=jnp.float32).astype(table.dtype)


def land_rows(arrived, dst_local, length, dst_rows):
    live_slot = lax.broadcasted_iota(jnp.int32, (dst_local.shape[0], 1), 0) < length
    placer = (
        (dst_local[:, None] == lax.broadcasted_iota(jnp.int32, (1, dst_rows), 1)) & live_slot
    ).astype(jnp.bfloat16)
    return lax.dot_general(
        placer, arrived, (((0,), (0,)), ((), ())), preferred_element_type=jnp.float32
    )


def adjacency(src_local, dst_local, length, src_rows, dst_rows, block):
    total = jnp.zeros((dst_rows, src_rows), jnp.float32)
    for start in range(0, src_local.shape[0], block):
        src_part = src_local[start : start + block]
        dst_part = dst_local[start : start + block]
        live_slot = start + lax.broadcasted_iota(jnp.int32, (block, 1), 0) < length
        src_hot = (src_part[:, None] == lax.broadcasted_iota(jnp.int32, (1, src_rows), 1)).astype(
            jnp.bfloat16
        )
        dst_hot = (
            (dst_part[:, None] == lax.broadcasted_iota(jnp.int32, (1, dst_rows), 1)) & live_slot
        ).astype(jnp.bfloat16)
        total = total + lax.dot_general(
            dst_hot, src_hot, (((0,), (0,)), ((), ())), preferred_element_type=jnp.float32
        )
    return total.astype(jnp.bfloat16)


def attend_block(queries, label_block, key_table, value_table):
    block = queries.shape[0]
    width = queries.shape[1]
    heads = width // DH
    table_size = key_table.shape[0]
    repeats = jnp.sum(
        (label_block[:, :, None] == lax.broadcasted_iota(jnp.int32, (1, 1, table_size), 2)).astype(
            jnp.float32
        ),
        axis=1,
    )
    query_heads = queries.reshape(block, heads, DH)
    key_heads = key_table.reshape(table_size, heads, DH)
    value_heads = value_table.reshape(table_size, heads, DH)
    scores = jnp.einsum(
        "bhd,thd->bht", query_heads, key_heads, preferred_element_type=jnp.float32
    ) / math.sqrt(DH)
    present = (repeats > 0.0)[:, None, :]
    top_score = jnp.max(jnp.where(present, scores, -jnp.inf), axis=-1, keepdims=True)
    weights = repeats[:, None, :] * jnp.exp(jnp.where(present, scores - top_score, 0.0))
    probs = (weights / jnp.sum(weights, axis=-1, keepdims=True)).astype(jnp.bfloat16)
    mixed = jnp.einsum("bht,thd->bhd", probs, value_heads, preferred_element_type=jnp.float32)
    return mixed.reshape(block, width).astype(jnp.bfloat16)


def shards(
    grid_in,
    mesh_embed,
    g2m_src,
    g2m_dst,
    g2m_own_src,
    g2m_own_dst,
    g2m_len,
    mesh_nbr,
    halo_rows,
    m2g_src,
    m2g_dst,
    m2g_own_src,
    m2g_own_dst,
    m2g_len,
    w_embed,
    w_send,
    w_mesh,
    attn_gain,
    w_query,
    w_key,
    w_value,
    w_project,
    mlp_gain,
    w_up,
    w_down,
    w_return,
    w_grid,
    w_skip,
    w_out,
):
    member_in = grid_in[0]
    grid_rows = member_in.shape[0]
    mesh_rows = mesh_embed.shape[0]
    width = mesh_embed.shape[1]
    edge_block = grid_rows // 2
    band = lax.axis_index("space")
    bands = lax.axis_size("space")
    upper = jnp.minimum(band + 1, bands - 1)
    lower = jnp.maximum(band - 1, 0)
    has_lower = band > 0
    has_upper = band < bands - 1
    grid_latent = jax.nn.silu(
        jnp.dot(member_in, w_embed, preferred_element_type=jnp.float32)
    ).astype(jnp.bfloat16)
    send_rows = jnp.dot(grid_latent, w_send, preferred_element_type=jnp.float32).astype(
        jnp.bfloat16
    )
    rows_up = g2m_src[0][upper]
    rows_down = g2m_src[0][lower]
    from_below = from_behind(pick_rows(send_rows, rows_up), "space", 1)
    from_above = from_behind(pick_rows(send_rows, rows_down), "space", -1)
    g2m_column = g2m_len[:, 0]
    own_links = adjacency(
        g2m_own_src[0], g2m_own_dst[0], g2m_column[band], grid_rows, mesh_rows, edge_block
    )
    mesh_agg = jnp.dot(own_links, send_rows, preferred_element_type=jnp.float32)
    mesh_agg = mesh_agg + land_rows(
        from_below, g2m_dst[0][lower], jnp.where(has_lower, g2m_column[lower], 0), mesh_rows
    )
    mesh_agg = mesh_agg + land_rows(
        from_above, g2m_dst[0][upper], jnp.where(has_upper, g2m_column[upper], 0), mesh_rows
    )
    gathered = (
        lax.all_gather(w_query, "member", axis=0, tiled=True),
        lax.all_gather(w_key, "member", axis=0, tiled=True),
        lax.all_gather(w_value, "member", axis=0, tiled=True),
        lax.all_gather(w_project, "member", axis=0, tiled=True),
        lax.all_gather(w_up, "member", axis=0, tiled=True),
        lax.all_gather(w_down, "member", axis=0, tiled=True),
    )
    full_query, full_key, full_value, full_project, full_up, full_down = gathered
    update = jax.nn.silu(
        jnp.dot(mesh_agg.astype(jnp.bfloat16), w_mesh, preferred_element_type=jnp.float32)
    )
    mesh_state = (mesh_embed.astype(jnp.float32) + update).astype(jnp.bfloat16)
    normed = layer_norm(mesh_state.astype(jnp.float32), attn_gain).astype(jnp.bfloat16)
    queries = jnp.dot(normed, full_query, preferred_element_type=jnp.float32).astype(jnp.bfloat16)
    key_local = jnp.dot(normed, full_key, preferred_element_type=jnp.float32).astype(jnp.bfloat16)
    value_local = jnp.dot(normed, full_value, preferred_element_type=jnp.float32).astype(
        jnp.bfloat16
    )
    published = halo_rows[0]
    far_normed = lax.all_gather(pick_rows(normed, published), "space", axis=0, tiled=True)
    far_keys = jnp.dot(far_normed, full_key, preferred_element_type=jnp.float32).astype(
        jnp.bfloat16
    )
    far_values = jnp.dot(far_normed, full_value, preferred_element_type=jnp.float32).astype(
        jnp.bfloat16
    )
    key_table = jnp.concatenate([key_local, far_keys], axis=0)
    value_table = jnp.concatenate([value_local, far_values], axis=0)
    own_rows = lax.broadcasted_iota(jnp.int32, (mesh_rows, 1), 0)
    label_all = jnp.concatenate([own_rows, mesh_nbr], axis=1)
    block = min(512, mesh_rows)
    count = mesh_rows // block

    def run_block(item):
        query_block, label_block = item
        return attend_block(query_block, label_block, key_table, value_table)

    attended = lax.map(
        run_block, (queries.reshape(count, block, width), label_all.reshape(count, block, -1))
    ).reshape(mesh_rows, width)
    after_attn = mesh_state.astype(jnp.float32) + jnp.dot(
        attended, full_project, preferred_element_type=jnp.float32
    )
    normed_two = layer_norm(after_attn, mlp_gain).astype(jnp.bfloat16)
    expanded = jax.nn.silu(jnp.dot(normed_two, full_up, preferred_element_type=jnp.float32)).astype(
        jnp.bfloat16
    )
    mesh_out = (
        after_attn + jnp.dot(expanded, full_down, preferred_element_type=jnp.float32)
    ).astype(jnp.bfloat16)
    return_rows = jnp.dot(mesh_out, w_return, preferred_element_type=jnp.float32).astype(
        jnp.bfloat16
    )
    back_below = from_behind(pick_rows(return_rows, m2g_src[0][upper]), "space", 1)
    back_above = from_behind(pick_rows(return_rows, m2g_src[0][lower]), "space", -1)
    m2g_column = m2g_len[:, 0]
    back_links = adjacency(
        m2g_own_src[0], m2g_own_dst[0], m2g_column[band], mesh_rows, grid_rows, edge_block
    )
    grid_agg = jnp.dot(back_links, return_rows, preferred_element_type=jnp.float32)
    grid_agg = grid_agg + land_rows(
        back_below, m2g_dst[0][lower], jnp.where(has_lower, m2g_column[lower], 0), grid_rows
    )
    grid_agg = grid_agg + land_rows(
        back_above, m2g_dst[0][upper], jnp.where(has_upper, m2g_column[upper], 0), grid_rows
    )
    pre = jnp.dot(grid_agg.astype(jnp.bfloat16), w_grid, preferred_element_type=jnp.float32)
    pre = pre + jnp.dot(grid_latent, w_skip, preferred_element_type=jnp.float32)
    updated = jax.nn.silu(pre).astype(jnp.bfloat16)
    result = lax.dot_general(
        w_out, updated, (((0,), (1,)), ((), ())), preferred_element_type=jnp.float32
    )
    return result.astype(jnp.bfloat16)[None]


def solution(mesh):
    placed = (
        P("member", "space", None),
        P("space", None),
        P("space", None, None),
        P("space", None, None),
        P("space", None),
        P("space", None),
        P(None, "space"),
        P("space", None),
        P("space", None),
        P("space", None, None),
        P("space", None, None),
        P("space", None),
        P("space", None),
        P(None, "space"),
        P(),
        P(),
        P(),
        P(),
        P("member", None),
        P("member", None),
        P("member", None),
        P("member", None),
        P(),
        P("member", None),
        P("member", None),
        P(),
        P(),
        P(),
        P(),
    )
    return jax.shard_map(
        shards, mesh=mesh, in_specs=placed, out_specs=P("member", None, "space"), check_vma=False
    )
```

profile of v0, /device:TPU:1, one launch (start us, length us, event | category | flops | bytes accessed | tf_op | source)
XLA Modules:
  0.0 155.0 jit_solution(43327420893235479)
XLA Ops:
  6.5 0.7 all-gather.3.cloned.1.call-update
  7.3 1.4 constant_dynamic-slice_fusion.6
  8.7 1.7 %multiply_convert_fusion.2 = bf16[1024,512]{1,0:T(8,128)(2,1)S(1)} fusion(bf16[256,512]{1,0:T(8,128)(2,1)} %param.43, bf16[1,1024,256]{2,1,0:T(8,128)(2,1)S(1)} %copy-done), kind=kOutput, calls=%fused_computation.6 | convolution fusion | flops 271056896 | bytes 1835008 | tf_op jit(solution)/shard_map/dot_general | solution.py:129
  10.4 0.7 convolution_convert_fusion
  11.2 1.2 convolution_convert_fusion.9
  12.4 4.7 %collective-permute-start = (bf16[256,512]{1,0:T(8,128)(2,1)}, bf16[256,512]{1,0:T(8,128)(2,1)}, u32[]{:S(2)}, u32[]{:S(2)}) collective-permute-start(bf16[256,512]{1,0:T(8,128)(2,1)} %convolution_convert_fusion.9), channel_id=1, source_target_pairs={{0,1},{1,2},{2,3},{3,4},{4,5},{5,6},{6,7},{8,9},{9,10},{10,11},{11... | collective-permute-start | bytes 786440 | tf_op jit(solution)/shard_map/ppermute | solution.py:17
  17.2 1.2 convolution_convert_fusion.8
  18.4 1.9 %collective-permute-start.1 = (bf16[256,512]{1,0:T(8,128)(2,1)}, bf16[256,512]{1,0:T(8,128)(2,1)}, u32[]{:S(2)}, u32[]{:S(2)}) collective-permute-start(bf16[256,512]{1,0:T(8,128)(2,1)} %convolution_convert_fusion.8), channel_id=1, source_target_pairs={{1,0},{2,1},{3,2},{4,3},{5,4},{6,5},{7,6},{9,8},{10,9},{11,10},{12... | collective-permute-start | bytes 786440 | tf_op jit(solution)/shard_map/ppermute | solution.py:17
  20.4 0.7 constant_dynamic-slice_fusion.1
  21.0 0.6 iota_compare_fusion.48
  21.7 0.6 fusion.137
  22.3 0.6 fusion.135
  23.0 0.6 iota_compare_fusion.49
  23.6 0.6 fusion.138
  24.2 0.6 fusion.136
  24.7 0.6 add_compare_fusion.1
  25.3 1.2 add_compare_fusion
  27.2 0.6 iota_compare_fusion.53
  28.9 12.3 %all_gather.23 = bf16[512,512]{1,0:T(8,128)(2,1)S(1)} all-gather(bf16[128,512]{1,0:T(8,128)(2,1)S(1)} %copy-done.2), channel_id=1, replica_groups=mesh['member'=4,'space'=8] {'member'}, dimensions={0}, use_global_device_ids=true | all-gather | bytes 655360 | tf_op jit(solution)/shard_map/all_gather | solution.py:151
  41.3 11.3 %all_gather.24 = bf16[512,512]{1,0:T(8,128)(2,1)} all-gather(bf16[128,512]{1,0:T(8,128)(2,1)S(1)} %copy-done.3), channel_id=1, replica_groups=mesh['member'=4,'space'=8] {'member'}, dimensions={0}, use_global_device_ids=true | all-gather | bytes 655360 | tf_op jit(solution)/shard_map/all_gather | solution.py:150
  52.6 1.6 %convert_reduce_fusion = f32[256,384]{1,0:T(8,128)S(1)} fusion(s32[256,33]{0,1:T(8,128)S(1)} %pad_add_fusion), kind=kLoop, calls=%fused_computation.1 | loop fusion | flops 9633792 | bytes 427008 | tf_op jit(solution)/shard_map/while/body/eval_jaxpr/reduce_sum | solution.py:66
  55.0 0.6 iota_compare_fusion.51
  56.2 0.6 iota_compare_fusion.50
  56.8 0.8 fusion.16
  57.6 1.9 %fusion.2 = f32[1024,256]{1,0:T(8,128)} fusion(s32[512]{0:T(512)S(1)} %bitcast.116, pred[512]{0:T(512)(128)(4,1)S(1)} %iota_compare_fusion.49, s32[512]{0:T(512)S(1)} %bitcast.117), kind=kOutput, calls=%fused_computation.16 | convolution fusion | flops 269615104 | bytes 1053184 | tf_op jit(solution)/shard_map/dot_general | solution.py:55
  59.5 0.8 fusion.25
  60.3 2.3 %fusion.46 = f32[256,512]{1,0:T(8,128)S(1)} fusion(bf16[1024,512]{1,0:T(8,128)(2,1)} %copy-done.27, f32[256,1024]{1,0:T(8,128)S(1)} %fusion.25, s32[512]{0:T(512)S(1)} %bitcast.119, s32[512]{0:T(512)S(1)} %bitcast.118, pred[512]{0:T(512)(128)(4,1)S(1)} %fusion.135), kind=kOutput, calls=%fused_computation.48 | convolution fusion | flops 538181632 | bytes 2626048 | tf_op jit(solution)/shard_map/dot_general | solution.py:142
  62.7 2.3 %fusion.35 = f32[1024,256]{1,0:T(8,128)S(1)} fusion(f32[1024,256]{1,0:T(8,128)} %fusion.2, s32[512]{0:T(512)S(1)} %bitcast.113, pred[512]{0:T(512)(128)(4,1)S(1)} %fusion.138, s32[512]{0:T(512)S(1)} %bitcast.115), kind=kOutput, calls=%fused_computation.43 | convolution fusion | flops 269877248 | bytes 2101760 | tf_op jit(solution)/shard_map/dot_general | solution.py:55
  65.0 1.0 fusion.32
  65.9 2.0 %fusion.29 = f32[1024,256]{1,0:T(8,128)} fusion(f32[1024,256]{1,0:T(8,128)S(1)} %fusion.32, s32[512]{0:T(512)S(1)} %bitcast.110, pred[512]{0:T(512)(128)(4,1)S(1)} %add_compare_fusion.1, s32[512]{0:T(512)S(1)} %bitcast.112), kind=kOutput, calls=%fused_computation.41 | convolution fusion | flops 269877248 | bytes 2101760 | tf_op jit(solution)/shard_map/dot_general | solution.py:55
  67.9 8.4 %all_gather.21 = bf16[512,512]{1,0:T(8,128)(2,1)S(1)} all-gather(bf16[128,512]{1,0:T(8,128)(2,1)S(1)} %copy-done.4), channel_id=1, replica_groups=mesh['member'=4,'space'=8] {'member'}, dimensions={0}, use_global_device_ids=true | all-gather | bytes 655360 | tf_op jit(solution)/shard_map/all_gather | solution.py:152
  76.3 1.4 constant_dynamic-slice_fusion
  77.7 12.8 %all_gather.25 = bf16[512,512]{1,0:T(8,128)(2,1)S(1)} all-gather(bf16[128,512]{1,0:T(8,128)(2,1)S(1)} %copy-done.5), channel_id=1, replica_groups=mesh['member'=4,'space'=8] {'member'}, dimensions={0}, use_global_device_ids=true | all-gather | bytes 655360 | tf_op jit(solution)/shard_map/all_gather | solution.py:153
  91.0 2.1 %convolution_add_fusion.2 = f32[256,512]{1,0:T(8,128)} fusion(f32[256,512]{1,0:T(8,128)S(1)} %fusion.46, bf16[256,512]{1,0:T(8,128)(2,1)} %collective-permute-done, s32[256]{0:T(256)S(1)} %bitcast.108, pred[256]{0:T(512)(128)(4,1)S(1)} %copy-done.20), kind=kOutput, calls=%fused_computation.51 | convolution fusion | flops 67371008 | bytes 1312000 | tf_op jit(solution)/shard_map/dot_general | solution.py:38
  93.1 2.1 %convert_reduce_fusion.1 = (f32[256]{0:T(256)S(1)}, bf16[256,512]{1,0:T(8,128)(2,1)S(1)}) fusion(bf16[512,512]{1,0:T(8,128)(2,1)} %param.45, f32[256,512]{1,0:T(8,128)} %convolution_add_fusion.2, bf16[256,512]{1,0:T(8,128)(2,1)} %collective-permute-done.1, s32[256]{0:T(256)S(1)} %bitcast.122, pred[256]{0:T(512)(128)(4,1)S(1)} %copy-done.25, ...), kind=kOutput, calls=%fused_computation.94 | convolution fusion | flops 202899200 | bytes 1837312 | tf_op jit(solution)/shard_map/dot_general | solution.py:159
  95.7 20.8 %all_gather.22 = bf16[128,512]{1,0:T(8,128)(2,1)S(1)} all-gather(bf16[16,512]{1,0:T(8,128)(2,1)S(1)} %convolution_convert_fusion.12), channel_id=1, replica_groups=mesh['member'=4,'space'=8] {'space'}, dimensions={0}, use_global_device_ids=true | all-gather | bytes 147456 | tf_op jit(solution)/shard_map/all_gather | solution.py:169
  117.4 1.4 fusion.50
  119.7 0.7 fusion.153
  121.5 2.3 %fusion.101 = f32[256,2048]{1,0:T(8,128)S(1)} fusion(bf16[512,2048]{1,0:T(8,128)(2,1)} %all-gather.3.cloned.1.call-done, f32[256,512]{1,0:T(8,128)S(1)} %get-tuple-element.58, f32[512]{0:T(512)S(1)} %copy-done.9, f32[256]{0:T(256)S(1)} %add_rsqrt_fusion, f32[256]{0:T(256)S(1)} %broadcast_multiply_fusion), kind=kOutput, calls=%fused_computation.126 | convolution fusion | flops 537395200 | bytes 4722688 | tf_op jit(solution)/shard_map/dot_general | solution.py:194
  123.9 2.6 %convolution_convert_fusion.3 = bf16[256,512]{1,0:T(8,128)(2,1)S(1)} fusion(bf16[512,512]{1,0:T(8,128)(2,1)} %param.54, f32[256,512]{1,0:T(8,128)S(1)} %get-tuple-element.58, bf16[2048,512]{1,0:T(8,128)(2,1)} %all-gather.5.cloned.1.call-done, f32[256,2048]{1,0:T(8,128)S(1)} %fusion.101), kind=kOutput, calls=%fused_computation.56 | convolution fusion | flops 674103296 | bytes 5505024 | tf_op jit(solution)/shard_map/dot_general | solution.py:200
  126.5 1.0 convolution_convert_fusion.2
  127.5 3.5 %collective-permute-start.2 = (bf16[256,512]{1,0:T(8,128)(2,1)}, bf16[256,512]{1,0:T(8,128)(2,1)}, u32[]{:S(2)}, u32[]{:S(2)}) collective-permute-start(bf16[256,512]{1,0:T(8,128)(2,1)} %convolution_convert_fusion.2), channel_id=1, source_target_pairs={{0,1},{1,2},{2,3},{3,4},{4,5},{5,6},{6,7},{8,9},{9,10},{10,11},{11... | collective-permute-start | bytes 786440 | tf_op jit(solution)/shard_map/ppermute | solution.py:17
  131.0 1.0 convolution_convert_fusion.1
  132.0 1.9 %collective-permute-start.3 = (bf16[256,512]{1,0:T(8,128)(2,1)}, bf16[256,512]{1,0:T(8,128)(2,1)}, u32[]{:S(2)}, u32[]{:S(2)}) collective-permute-start(bf16[256,512]{1,0:T(8,128)(2,1)} %convolution_convert_fusion.1), channel_id=1, source_target_pairs={{1,0},{2,1},{3,2},{4,3},{5,4},{6,5},{7,6},{9,8},{10,9},{11,10},{12... | collective-permute-start | bytes 786440 | tf_op jit(solution)/shard_map/ppermute | solution.py:17
  133.9 2.6 %fusion.44 = f32[1024,512]{1,0:T(8,128)S(1)} fusion(bf16[256,512]{1,0:T(8,128)(2,1)S(1)} %convolution_convert_fusion.3, f32[1024,256]{1,0:T(8,128)} %fusion.29, s32[512]{0:T(512)S(1)} %bitcast.103, pred[512]{0:T(512)(128)(4,1)S(1)} %copy-done.17, s32[512]{0:T(512)S(1)} %bitcast.104), kind=kOutput, calls=%fused_computation.47 | convolution fusion | flops 538574848 | bytes 3412480 | tf_op jit(solution)/shard_map/dot_general | solution.py:209
  136.6 2.9 %fusion.71 = f32[1024,512]{1,0:T(8,128)} fusion(bf16[256,512]{1,0:T(8,128)(2,1)} %collective-permute-done.2, s32[256]{0:T(256)S(1)} %bitcast.105, pred[256]{0:T(512)(128)(4,1)S(1)} %copy-done.19), kind=kOutput, calls=%fused_computation.90 | convolution fusion | flops 268959744 | bytes 2360576 | tf_op jit(solution)/shard_map/dot_general | solution.py:38
  140.0 4.2 %fusion.23 = f32[1024,512]{1,0:T(8,128)} fusion(bf16[512,512]{1,0:T(8,128)(2,1)S(1)} %copy-done.1, f32[1024,512]{1,0:T(8,128)S(1)} %fusion.44, f32[1024,512]{1,0:T(8,128)} %fusion.71, bf16[256,512]{1,0:T(8,128)(2,1)} %collective-permute-done.3, s32[256]{0:T(256)S(1)} %bitcast.109, pred[256]{0:T(512)(128)(4,1)S(1)} %copy-done.18), kind=kOutput, calls=%fused_computation.37 | convolution fusion | flops 807403520 | bytes 7079168 | tf_op jit(solution)/shard_map/dot_general | solution.py:216
  144.2 4.0 %fusion.52 = bf16[1,84,1024]{2,1,0:T(8,128)(2,1)} fusion(bf16[512,84]{0,1:T(8,128)(2,1)S(1)} %copy-done.22, f32[1024,512]{1,0:T(8,128)} %fusion.23, bf16[1024,512]{1,0:T(8,128)(2,1)} %copy-done.26, bf16[512,512]{1,0:T(8,128)(2,1)} %param.56), kind=kOutput, calls=%fused_computation.69 | convolution fusion | flops 628183040 | bytes 3928064 | tf_op jit(solution)/shard_map/dot_general | solution.py:219
  (91 shorter events, 5.0 us)
Async XLA Ops:
  6.5 2.1 %copy-start = (bf16[1,1024,256]{2,1,0:T(8,128)(2,1)S(1)}, bf16[1,1024,256]{2,1,0:T(8,128)(2,1)}, u32[]{:S(2)}) copy-start(bf16[1,1024,256]{2,1,0:T(8,128)(2,1)} %param.29) | copy-start | bytes 1572868
  6.5 114.9 %all-gather.3.cloned.1.call-start = ((), (), s32[]{:S(2)}) async-start(), calls=%async_computation | async-start | bytes 2621440 | tf_op jit(solution)/shard_map/all_gather | solution.py:154
  7.3 116.6 %all-gather.5.cloned.1.call-start = ((), (), s32[]{:S(2)}) async-start(), calls=%async_computation.1 | async-start | bytes 2621440 | tf_op jit(solution)/shard_map/all_gather | solution.py:155
  8.7 1.7 %copy-start.21 = (bf16[512,512]{1,0:T(8,128)(2,1)S(1)}, bf16[512,512]{1,0:T(8,128)(2,1)}, u32[]{:S(2)}) copy-start(bf16[512,512]{1,0:T(8,128)(2,1)} %param.44) | copy-start | bytes 1572868
  10.4 2.0 %copy-start.26 = (bf16[1024,512]{1,0:T(8,128)(2,1)}, bf16[1024,512]{1,0:T(8,128)(2,1)S(1)}, u32[]{:S(2)}) copy-start(bf16[1024,512]{1,0:T(8,128)(2,1)S(1)} %multiply_convert_fusion.2) | copy-start | bytes 3145732
  11.1 7.3 %copy-start.27 = (bf16[1024,512]{1,0:T(8,128)(2,1)}, bf16[1024,512]{1,0:T(8,128)(2,1)S(1)}, u32[]{:S(2)}) copy-start(bf16[1024,512]{1,0:T(8,128)(2,1)S(1)} %convolution_convert_fusion) | copy-start | bytes 3145732
  11.1 9.2 %copy-start.12 = (s32[8,1]{0,1:T(1,128)S(1)}, s32[8,1]{0,1:T(1,128)}, u32[]{:S(2)}) copy-start(s32[8,1]{0,1:T(1,128)} %param.42) | copy-start | bytes 100
  11.1 9.2 %copy-start.13 = (s32[8,1]{0,1:T(1,128)S(1)}, s32[8,1]{0,1:T(1,128)}, u32[]{:S(2)}) copy-start(s32[8,1]{0,1:T(1,128)} %param.35) | copy-start | bytes 100
  11.2 15.3 %copy-start.10 = (s32[1,1536]{1,0:T(1,128)S(1)}, s32[1,1536]{1,0:T(1,128)}, u32[]{:S(2)}) copy-start(s32[1,1536]{1,0:T(1,128)} %param.34) | copy-start | bytes 18436
  11.2 15.3 %copy-start.11 = (s32[1,1536]{1,0:T(1,128)S(1)}, s32[1,1536]{1,0:T(1,128)}, u32[]{:S(2)}) copy-start(s32[1,1536]{1,0:T(1,128)} %param.33) | copy-start | bytes 18436
  11.2 17.8 %copy-start.2 = (bf16[128,512]{1,0:T(8,128)(2,1)S(1)}, bf16[128,512]{1,0:T(8,128)(2,1)}, u32[]{:S(2)}) copy-start(bf16[128,512]{1,0:T(8,128)(2,1)} %param.48) | copy-start | bytes 393220
  11.2 30.1 %copy-start.3 = (bf16[128,512]{1,0:T(8,128)(2,1)S(1)}, bf16[128,512]{1,0:T(8,128)(2,1)}, u32[]{:S(2)}) copy-start(bf16[128,512]{1,0:T(8,128)(2,1)} %param.47) | copy-start | bytes 393220
  12.4 40.1 %copy-start.6 = (s32[256,32]{0,1:T(8,128)S(1)}, s32[256,32]{0,1:T(8,128)}, u32[]{:S(2)}) copy-start(s32[256,32]{0,1:T(8,128)} %param.36) | copy-start | bytes 98308
  12.4 78.5 %collective-permute-start = (bf16[256,512]{1,0:T(8,128)(2,1)}, bf16[256,512]{1,0:T(8,128)(2,1)}, u32[]{:S(2)}, u32[]{:S(2)}) collective-permute-start(bf16[256,512]{1,0:T(8,128)(2,1)} %convolution_convert_fusion.9), channel_id=1, source_target_pairs={{0,1},{1,2},{2,3},{3,4},{4,5},{5,6},{6,7},{8,9},{9,10},{10,11},{11... | collective-permute-start | bytes 786440 | tf_op jit(solution)/shard_map/ppermute | solution.py:17
  17.2 37.1 %copy-start.7 = (s32[1,2560]{1,0:T(1,128)S(1)}, s32[1,2560]{1,0:T(1,128)}, u32[]{:S(2)}) copy-start(s32[1,2560]{1,0:T(1,128)} %param.41) | copy-start | bytes 30724
  17.2 37.1 %copy-start.8 = (s32[1,2560]{1,0:T(1,128)S(1)}, s32[1,2560]{1,0:T(1,128)}, u32[]{:S(2)}) copy-start(s32[1,2560]{1,0:T(1,128)} %param.40) | copy-start | bytes 30724
  18.4 74.7 %collective-permute-start.1 = (bf16[256,512]{1,0:T(8,128)(2,1)}, bf16[256,512]{1,0:T(8,128)(2,1)}, u32[]{:S(2)}, u32[]{:S(2)}) collective-permute-start(bf16[256,512]{1,0:T(8,128)(2,1)} %convolution_convert_fusion.8), channel_id=1, source_target_pairs={{1,0},{2,1},{3,2},{4,3},{5,4},{6,5},{7,6},{9,8},{10,9},{11,10},{12... | collective-permute-start | bytes 786440 | tf_op jit(solution)/shard_map/ppermute | solution.py:17
  64.9 3.0 %copy-start.4 = (bf16[128,512]{1,0:T(8,128)(2,1)S(1)}, bf16[128,512]{1,0:T(8,128)(2,1)}, u32[]{:S(2)}) copy-start(bf16[128,512]{1,0:T(8,128)(2,1)} %param.49) | copy-start | bytes 393220
  64.9 12.8 %copy-start.5 = (bf16[128,512]{1,0:T(8,128)(2,1)S(1)}, bf16[128,512]{1,0:T(8,128)(2,1)}, u32[]{:S(2)}) copy-start(bf16[128,512]{1,0:T(8,128)(2,1)} %param.50) | copy-start | bytes 393220
  65.9 25.0 %copy-start.20 = (pred[256]{0:T(512)(128)(4,1)S(1)}, pred[256]{0:T(512)(128)(4,1)}, u32[]{:S(2)}) copy-start(pred[256]{0:T(512)(128)(4,1)} %iota_compare_fusion.53) | copy-start | bytes 772
  67.9 25.2 %copy-start.16 = (s32[1,1,256]{2,1,0:T(1,128)S(1)}, s32[1,1,256]{2,1,0:T(1,128)}, u32[]{:S(2)}) copy-start(s32[1,1,256]{2,1,0:T(1,128)} %get-tuple-element.65) | copy-start | bytes 3076
  67.9 25.2 %copy-start.25 = (pred[256]{0:T(512)(128)(4,1)S(1)}, pred[256]{0:T(512)(128)(4,1)}, u32[]{:S(2)}) copy-start(pred[256]{0:T(512)(128)(4,1)} %iota_compare_fusion.52) | copy-start | bytes 772
  93.1 2.4 %copy-start.23 = (f32[512]{0:T(512)S(1)}, f32[512]{0:T(512)}, u32[]{:S(2)}) copy-start(f32[512]{0:T(512)} %param.46) | copy-start | bytes 6148
  93.1 2.4 %copy-start.24 = (s32[1,16]{1,0:T(1,128)S(1)}, s32[1,16]{1,0:T(1,128)}, u32[]{:S(2)}) copy-start(s32[1,16]{1,0:T(1,128)} %param.37) | copy-start | bytes 196
  120.8 0.7 copy-start.9
  123.8 2.7 %copy-start.14 = (s32[1,1,256]{2,1,0:T(1,128)S(1)}, s32[1,1,256]{2,1,0:T(1,128)}, u32[]{:S(2)}) copy-start(s32[1,1,256]{2,1,0:T(1,128)} %get-tuple-element.36) | copy-start | bytes 3076
  123.8 10.1 %copy-start.17 = (pred[512]{0:T(512)(128)(4,1)S(1)}, pred[512]{0:T(512)(128)(4,1)}, u32[]{:S(2)}) copy-start(pred[512]{0:T(512)(128)(4,1)} %add_compare_fusion) | copy-start | bytes 1540
  127.5 9.1 %copy-start.19 = (pred[256]{0:T(512)(128)(4,1)S(1)}, pred[256]{0:T(512)(128)(4,1)}, u32[]{:S(2)}) copy-start(pred[256]{0:T(512)(128)(4,1)} %iota_compare_fusion.51) | copy-start | bytes 772
  127.5 9.1 %collective-permute-start.2 = (bf16[256,512]{1,0:T(8,128)(2,1)}, bf16[256,512]{1,0:T(8,128)(2,1)}, u32[]{:S(2)}, u32[]{:S(2)}) collective-permute-start(bf16[256,512]{1,0:T(8,128)(2,1)} %convolution_convert_fusion.2), channel_id=1, source_target_pairs={{0,1},{1,2},{2,3},{3,4},{4,5},{5,6},{6,7},{8,9},{9,10},{10,11},{11... | collective-permute-start | bytes 786440 | tf_op jit(solution)/shard_map/ppermute | solution.py:17
  132.0 8.0 %collective-permute-start.3 = (bf16[256,512]{1,0:T(8,128)(2,1)}, bf16[256,512]{1,0:T(8,128)(2,1)}, u32[]{:S(2)}, u32[]{:S(2)}) collective-permute-start(bf16[256,512]{1,0:T(8,128)(2,1)} %convolution_convert_fusion.1), channel_id=1, source_target_pairs={{1,0},{2,1},{3,2},{4,3},{5,4},{6,5},{7,6},{9,8},{10,9},{11,10},{12... | collective-permute-start | bytes 786440 | tf_op jit(solution)/shard_map/ppermute | solution.py:17
  133.9 6.1 %copy-start.1 = (bf16[512,512]{1,0:T(8,128)(2,1)S(1)}, bf16[512,512]{1,0:T(8,128)(2,1)}, u32[]{:S(2)}) copy-start(bf16[512,512]{1,0:T(8,128)(2,1)} %param.55) | copy-start | bytes 1572868
  133.9 6.1 %copy-start.15 = (s32[1,1,256]{2,1,0:T(1,128)S(1)}, s32[1,1,256]{2,1,0:T(1,128)}, u32[]{:S(2)}) copy-start(s32[1,1,256]{2,1,0:T(1,128)} %get-tuple-element.60) | copy-start | bytes 3076
  133.9 6.1 %copy-start.18 = (pred[256]{0:T(512)(128)(4,1)S(1)}, pred[256]{0:T(512)(128)(4,1)}, u32[]{:S(2)}) copy-start(pred[256]{0:T(512)(128)(4,1)} %iota_compare_fusion.50) | copy-start | bytes 772
  140.0 4.2 %copy-start.22 = (bf16[512,84]{0,1:T(8,128)(2,1)S(1)}, bf16[512,84]{0,1:T(8,128)(2,1)}, u32[]{:S(2)}) copy-start(bf16[512,84]{0,1:T(8,128)(2,1)} %param.57) | copy-start | bytes 258052
Sparse Core Ops, SparseCore 0:
  9.2 41.5 all-gather.2
  52.7 41.1 all-gather.4
where the time goes:
time: 156 us; the launch traced here: 155 us
  blocking collectives  65.7 us (42%)
  matrix products  44.6 us (29%)
  between operations  16.7 us (11%)
  starting transfers between devices  12.1 us (8%)
  other arithmetic  10.5 us (7%)
  local copies, waits for them, and re-layouts  4.16 us (3%)
    all_gather x1, blocking collectives, shards(): lax.all_gather(pick_rows(normed, published), 'space', axis=0, tiled=True)  20.8 us
    all_gather x1, blocking collectives, shards(): lax.all_gather(w_project, 'member', axis=0, tiled=True)  12.8 us
    all_gather x1, blocking collectives, shards(): lax.all_gather(w_key, 'member', axis=0, tiled=True)  12.3 us
    ppermute x4, starting transfers between devices, from_behind(): return lax.ppermute(block, axis, route)  12 us
    all_gather x1, blocking collectives, shards(): lax.all_gather(w_query, 'member', axis=0, tiled=True)  11.3 us
    dot_general x6, matrix products, adjacency(): lax.dot_general(dst_hot, src_hot, (((0,), (0,)), ((), ())), preferred_ele...  8.68 us
    all_gather x1, blocking collectives, shards(): lax.all_gather(w_value, 'member', axis=0, tiled=True)  8.43 us
    lt x8, other arithmetic, adjacency(): live_slot = start + lax.broadcasted_iota(jnp.int32, (block, 1), 0) < length  5.39 us
  transfers between devices with their start and end apart: 6, of which 1 were waited for; matrix products, arithmetic and copies ran while one was open for 31% of the time, Pallas kernels for 0%

commit v1 on v0

v1 whole, which is shorter than its diff:
```python
import functools
import math

import jax
import jax.numpy as jnp
from jax import lax
from jax.experimental import pallas as pl
from jax.experimental.pallas import tpu as pltpu
from jax.sharding import PartitionSpec as P

DH = 128
EPS = 1e-05
EDGE_BLOCK = 512
BF = jnp.bfloat16
F32 = jnp.float32
MESH = pl.DeviceIdType.MESH


def dot(a, b):
    return jnp.dot(a, b, preferred_element_type=F32)


def dot_nt(a, b):
    return lax.dot_general(a, b, (((1,), (1,)), ((), ())), preferred_element_type=F32)


def silu(v):
    return v / (1.0 + jnp.exp(-v))


def layer_norm(values, norm_gain):
    centred = values - jnp.mean(values, axis=-1, keepdims=True)
    spread = jnp.mean(centred * centred, axis=-1, keepdims=True)
    return centred * lax.rsqrt(spread + EPS) * norm_gain


def iota(shape, dim):
    return lax.broadcasted_iota(jnp.int32, shape, dim)


def one_hot_t(row, rows):
    return jnp.where(iota((rows, row.shape[1]), 0) == row, 1.0, 0.0).astype(BF)


def one_hot(row, rows):
    count = row.shape[1]
    spread = jnp.transpose(jnp.broadcast_to(row, (128, count)))
    lane = iota((count, 128), 1)
    parts = [
        jnp.where(spread == lane + start, 1.0, 0.0).astype(BF) for start in range(0, rows, 128)
    ]
    return jnp.concatenate(parts, axis=1)


def live(row, length, start=0):
    return jnp.where(iota(row.shape, 1) + start < length, row, -1)


def kernel(
    bands, grid_in, mesh_embed, g2m_src, g2m_dst, g2m_own_src, g2m_own_dst, g2m_len, mesh_nbr,
    halo_rows, m2g_src, m2g_dst, m2g_own_src, m2g_own_dst, m2g_len, w_embed, w_send, w_mesh,
    attn_gain, w_query, w_key, w_value, w_project, mlp_gain, w_up, w_down, w_return, w_grid,
    w_skip, w_out, out, attn_w, up_w, down_w, latent, sends, links, links_acc, back, back_acc,
    skip, pick_up, pick_dn, from_lo, from_hi, ret_up, ret_dn, back_lo, back_hi, far,
    wsend, wrecv, msend, mrecv, hsend, hrecv,
):
    me = lax.axis_index("member")
    band = lax.axis_index("space")
    xm = me + 1 - 2 * lax.rem(me, 2)
    ym = lax.rem(me + 2, 4)
    dm = 3 - me
    core = lax.rem(band, 2)
    mate = band + 1 - 2 * core
    has_lower = band > 0
    has_upper = band < bands - 1
    upper = jnp.minimum(band + 1, bands - 1)
    lower = jnp.maximum(band - 1, 0)
    grid_rows = grid_in.shape[1]
    mesh_rows, width = mesh_embed.shape
    hb = halo_rows.shape[1]

    barrier = pltpu.get_barrier_semaphore()
    pl.semaphore_signal(barrier, inc=1, device_id=(xm, band), device_id_type=MESH)
    pl.semaphore_signal(barrier, inc=1, device_id=(ym, band), device_id_type=MESH)
    for off in range(1, bands):
        pl.semaphore_signal(
            barrier, inc=1, device_id=(me, lax.rem(band + off, bands)), device_id_type=MESH
        )
    for i, ref in enumerate((w_query, w_key, w_value, w_project)):
        attn_w[me, i] = ref[...]
    up_w[me] = w_up[...]
    down_w[me] = w_down[...]
    pl.semaphore_wait(barrier, bands + 1)

    def piece(group, slot, part):
        def rows(total):
            half = total // 2
            if part is None:
                return pl.ds(pl.multiple_of(core * half, half), half)
            quarter = half // 2
            return pl.ds(pl.multiple_of(core * half + part * quarter, quarter), quarter)

        if group == 0:
            return attn_w.at[slot, :, rows(attn_w.shape[2])]
        buf = up_w if group == 1 else down_w
        return buf.at[slot, rows(buf.shape[1])]

    def wcopy(group, kind):
        slot, part, target = {
            "a": (me, None, (xm, band)),
            "b": (me, None, (ym, band)),
            "c": (xm, 0, (ym, band)),
            "d": (ym, 1, (xm, band)),
            "e": (xm, None, (me, mate)),
            "f": (ym, None, (me, mate)),
            "g": (dm, None, (me, mate)),
        }[kind]
        k = "abcdefg".index(kind)
        ref = piece(group, slot, part)
        return pltpu.make_async_remote_copy(
            src_ref=ref, dst_ref=ref, send_sem=wsend.at[group, k], recv_sem=wrecv.at[group, k],
            device_id=target, device_id_type=MESH,
        )

    def wstart(group, kinds):
        for kind in kinds:
            wcopy(group, kind).start()

    def wwait(group, kinds):
        for kind in kinds:
            wcopy(group, kind).wait_recv()

    def message(k, src, dst, target):
        return pltpu.make_async_remote_copy(
            src_ref=src, dst_ref=dst, send_sem=msend.at[k], recv_sem=mrecv.at[k],
            device_id=(me, target), device_id_type=MESH,
        )

    wstart(0, "ab")

    block = 256

    def embed(i, carry):
        rows = pl.ds(pl.multiple_of(i * block, block), block)
        lat = silu(dot(grid_in[0, rows, :], w_embed[...])).astype(BF)
        latent[rows, :] = lat
        sends[rows, :] = dot(lat, w_send[...]).astype(BF)
        return carry

    lax.fori_loop(0, grid_rows // block, embed, 0)
    pick_up[...] = dot(one_hot(g2m_src[0, pl.ds(upper, 1), :], grid_rows), sends[...]).astype(BF)
    pick_dn[...] = dot(one_hot(g2m_src[0, pl.ds(lower, 1), :], grid_rows), sends[...]).astype(BF)

    @pl.when(has_upper)
    def _():
        message(0, pick_up, from_lo, upper).start()

    @pl.when(has_lower)
    def _():
        message(1, pick_dn, from_hi, lower).start()

    wwait(0, "ab")
    wstart(0, "cdef")
    wstart(1, "ab")

    links_acc[...] = jnp.zeros_like(links_acc)
    own_length = g2m_len[band, 0]

    def own_links(i, carry):
        start = pl.multiple_of(i * EDGE_BLOCK, EDGE_BLOCK)
        dst = live(g2m_own_dst[:, pl.ds(start, EDGE_BLOCK)], own_length, start)
        src = g2m_own_src[:, pl.ds(start, EDGE_BLOCK)]
        links_acc[...] += dot_nt(one_hot_t(dst, mesh_rows), one_hot_t(src, grid_rows))
        return carry

    lax.fori_loop(0, g2m_own_src.shape[1] // EDGE_BLOCK, own_links, 0)
    links[...] = links_acc[...].astype(BF)
    mesh_agg = dot(links[...], sends[...])

    wwait(0, "cd")
    wstart(0, "g")
    wwait(1, "ab")
    wstart(1, "cdef")
    wstart(2, "ab")

    @pl.when(has_lower)
    def _():
        message(0, pick_up, from_lo, upper).wait_recv()

    @pl.when(has_upper)
    def _():
        message(1, pick_dn, from_hi, lower).wait_recv()

    @pl.when(jnp.logical_not(has_lower))
    def _():
        from_lo[...] = jnp.zeros_like(from_lo)

    @pl.when(jnp.logical_not(has_upper))
    def _():
        from_hi[...] = jnp.zeros_like(from_hi)

    len_lo = jnp.where(has_lower, g2m_len[lower, 0], 0)
    len_hi = jnp.where(has_upper, g2m_len[upper, 0], 0)
    place_lo = one_hot_t(live(g2m_dst[0, pl.ds(lower, 1), :], len_lo), mesh_rows)
    place_hi = one_hot_t(live(g2m_dst[0, pl.ds(upper, 1), :], len_hi), mesh_rows)
    mesh_agg = mesh_agg + dot(place_lo, from_lo[...]) + dot(place_hi, from_hi[...])
    update = silu(dot(mesh_agg.astype(BF), w_mesh[...]))
    mesh_state = (mesh_embed[...].astype(F32) + update).astype(BF)
    normed = layer_norm(mesh_state.astype(F32), attn_gain[...].reshape(1, width)).astype(BF)

    wanted = jnp.zeros((hb, mesh_rows), jnp.int32)
    for j in range(hb):
        wanted = jnp.where(iota((hb, mesh_rows), 0) == j, halo_rows[0, j], wanted)
    picker = jnp.where(wanted == iota((hb, mesh_rows), 1), 1.0, 0.0).astype(BF)
    own_far = pl.ds(pl.multiple_of(band * hb, hb), hb)
    far[own_far, :] = dot(picker, normed).astype(BF)

    def halo(off):
        rows = far.at[own_far]
        return pltpu.make_async_remote_copy(
            src_ref=rows, dst_ref=rows, send_sem=hsend.at[off], recv_sem=hrecv.at[off],
            device_id=(me, lax.rem(band + off, bands)), device_id_type=MESH,
        )

    def halo_in(off):
        rows = far.at[pl.ds(pl.multiple_of(lax.rem(band - off + bands, bands) * hb, hb), hb)]
        return pltpu.make_async_remote_copy(
            src_ref=rows, dst_ref=rows, send_sem=hsend.at[off], recv_sem=hrecv.at[off],
            device_id=(me, lax.rem(band + off, bands)), device_id_type=MESH,
        )

    for off in range(1, bands):
        halo(off).start()

    table = mesh_rows + bands * hb
    nbr = mesh_nbr[...]
    label = iota((mesh_rows, table), 1)
    repeats = jnp.where(label == iota((mesh_rows, table), 0), 1.0, 0.0)
    for k in range(nbr.shape[1]):
        repeats = repeats + jnp.where(nbr[:, k : k + 1] == label, 1.0, 0.0)

    wwait(0, "efg")

    def attn_full(i):
        return attn_w[:, i].reshape(width, width)

    queries = dot(normed, attn_full(0)).astype(BF)
    key_local = dot(normed, attn_full(1)).astype(BF)
    value_local = dot(normed, attn_full(2)).astype(BF)

    wwait(1, "cd")
    wstart(1, "g")
    wwait(2, "ab")
    wstart(2, "cdef")

    for off in range(1, bands):
        halo_in(off).wait_recv()
    keys = jnp.concatenate([key_local, dot(far[...], attn_full(1)).astype(BF)], axis=0)
    values = jnp.concatenate([value_local, dot(far[...], attn_full(2)).astype(BF)], axis=0)
    present = repeats > 0.0
    mixed = []
    for h in range(width // DH):
        cols = slice(h * DH, (h + 1) * DH)
        scores = dot_nt(queries[:, cols], keys[:, cols]) / math.sqrt(DH)
        top = jnp.max(jnp.where(present, scores, -jnp.inf), axis=-1, keepdims=True)
        weights = repeats * jnp.exp(jnp.where(present, scores - top, 0.0))
        probs = (weights / jnp.sum(weights, axis=-1, keepdims=True)).astype(BF)
        mixed.append(dot(probs, values[:, cols]).astype(BF))
    attended = jnp.concatenate(mixed, axis=1)
    after_attn = mesh_state.astype(F32) + dot(attended, attn_full(3))
    normed_two = layer_norm(after_attn, mlp_gain[...].reshape(1, width)).astype(BF)

    wwait(2, "cd")
    wstart(2, "g")

    back_acc[...] = jnp.zeros_like(back_acc)
    back_length = m2g_len[band, 0]

    def own_back(i, carry):
        start = pl.multiple_of(i * EDGE_BLOCK, EDGE_BLOCK)
        dst = live(m2g_own_dst[:, pl.ds(start, EDGE_BLOCK)], back_length, start)
        src = m2g_own_src[:, pl.ds(start, EDGE_BLOCK)]
        back_acc[...] += dot_nt(one_hot_t(dst, grid_rows), one_hot_t(src, mesh_rows))
        return carry

    lax.fori_loop(0, m2g_own_src.shape[1] // EDGE_BLOCK, own_back, 0)
    back[...] = back_acc[...].astype(BF)

    def skip_rows(i, carry):
        rows = pl.ds(pl.multiple_of(i * block, block), block)
        skip[rows, :] = dot(latent[rows, :], w_skip[...])
        return carry

    lax.fori_loop(0, grid_rows // block, skip_rows, 0)

    wwait(1, "efg")
    hidden = down_w.shape[1]
    expanded = []
    for j in range(down_w.shape[0]):
        up = up_w[:, :, j * hidden : (j + 1) * hidden].reshape(width, hidden)
        expanded.append(silu(dot(normed_two, up)).astype(BF))
    wwait(2, "efg")
    total = after_attn
    for j in range(down_w.shape[0]):
        total = total + dot(expanded[j], down_w[j])
    mesh_out = total.astype(BF)
    return_rows = dot(mesh_out, w_return[...]).astype(BF)
    ret_up[...] = dot(one_hot(m2g_src[0, pl.ds(upper, 1), :], mesh_rows), return_rows).astype(BF)
    ret_dn[...] = dot(one_hot(m2g_src[0, pl.ds(lower, 1), :], mesh_rows), return_rows).astype(BF)

    @pl.when(has_upper)
    def _():
        message(2, ret_up, back_lo, upper).start()

    @pl.when(has_lower)
    def _():
        message(3, ret_dn, back_hi, lower).start()

    agg = dot(back[...], return_rows)

    @pl.when(has_lower)
    def _():
        message(2, ret_up, back_lo, upper).wait_recv()

    @pl.when(has_upper)
    def _():
        message(3, ret_dn, back_hi, lower).wait_recv()

    @pl.when(jnp.logical_not(has_lower))
    def _():
        back_lo[...] = jnp.zeros_like(back_lo)

    @pl.when(jnp.logical_not(has_upper))
    def _():
        back_hi[...] = jnp.zeros_like(back_hi)

    blen_lo = jnp.where(has_lower, m2g_len[lower, 0], 0)
    blen_hi = jnp.where(has_upper, m2g_len[upper, 0], 0)
    land_lo = one_hot_t(live(m2g_dst[0, pl.ds(lower, 1), :], blen_lo), grid_rows)
    land_hi = one_hot_t(live(m2g_dst[0, pl.ds(upper, 1), :], blen_hi), grid_rows)
    agg = agg + dot(land_lo, back_lo[...]) + dot(land_hi, back_hi[...])
    pre = dot(agg.astype(BF), w_grid[...]) + skip[...]
    updated = silu(pre).astype(BF)
    f_out = w_out.shape[1]
    padded = jnp.concatenate(
        [w_out[...].astype(F32), jnp.zeros((width, 128 - f_out), F32)], axis=1
    )
    head = jnp.transpose(padded).astype(BF)
    out[...] = dot_nt(head, updated)[:f_out].astype(BF)

    for group in range(3):
        for kind in "abcdefg":
            wcopy(group, kind).wait_send()
    for off in range(1, bands):
        halo(off).wait_send()

    @pl.when(has_upper)
    def _():
        message(0, pick_up, from_lo, upper).wait_send()
        message(2, ret_up, back_lo, upper).wait_send()

    @pl.when(has_lower)
    def _():
        message(1, pick_dn, from_hi, lower).wait_send()
        message(3, ret_dn, back_hi, lower).wait_send()


SCALAR_ARGS = (6, 8, 13)


def shards(*args):
    grid_rows = args[0].shape[1]
    mesh_rows, width = args[1].shape
    slots = args[2].shape[2]
    hb = args[8].shape[1]
    bands = lax.axis_size("space")
    members = lax.axis_size("member")
    depth, ffn = args[23].shape
    down = args[24].shape
    f_out = args[28].shape[1]
    msg = pltpu.VMEM((slots, width), BF)
    in_specs = [
        pl.BlockSpec(memory_space=pltpu.SMEM if i in SCALAR_ARGS else pltpu.VMEM)
        for i in range(len(args))
    ]
    result = pl.pallas_call(
        functools.partial(kernel, bands),
        out_shape=jax.ShapeDtypeStruct((f_out, grid_rows), BF),
        in_specs=in_specs,
        out_specs=pl.BlockSpec(memory_space=pltpu.VMEM),
        scratch_shapes=[
            pltpu.VMEM((members, 4, depth, width), BF),
            pltpu.VMEM((members, depth, ffn), BF),
            pltpu.VMEM((members,) + tuple(down), BF),
            pltpu.VMEM((grid_rows, width), BF),
            pltpu.VMEM((grid_rows, width), BF),
            pltpu.VMEM((mesh_rows, grid_rows), BF),
            pltpu.VMEM((mesh_rows, grid_rows), F32),
            pltpu.VMEM((grid_rows, mesh_rows), BF),
            pltpu.VMEM((grid_rows, mesh_rows), F32),
            pltpu.VMEM((grid_rows, width), F32),
            msg, msg, msg, msg, msg, msg, msg, msg,
            pltpu.VMEM((bands * hb, width), BF),
            pltpu.SemaphoreType.DMA((3, 7)),
            pltpu.SemaphoreType.DMA((3, 7)),
            pltpu.SemaphoreType.DMA((4,)),
            pltpu.SemaphoreType.DMA((4,)),
            pltpu.SemaphoreType.DMA((bands,)),
            pltpu.SemaphoreType.DMA((bands,)),
        ],
        compiler_params=pltpu.CompilerParams(
            collective_id=0, has_side_effects=True, vmem_limit_bytes=52 * 1024 * 1024
        ),
        cost_estimate=pl.CostEstimate(
            flops=8_000_000_000, bytes_accessed=6_000_000, transcendentals=3_000_000
        ),
    )(*args)
    return result[None]


def solution(mesh):
    placed = (
        P("member", "space", None),
        P("space", None),
        P("space", None, None),
        P("space", None, None),
        P("space", None),
        P("space", None),
        P(None, "space"),
        P("space", None),
        P("space", None),
        P("space", None, None),
        P("space", None, None),
        P("space", None),
        P("space", None),
        P(None, "space"),
        P(),
        P(),
        P(),
        P(),
        P("member", None),
        P("member", None),
        P("member", None),
        P("member", None),
        P(),
        P("member", None),
        P("member", None),
        P(),
        P(),
        P(),
        P(),
    )
    return jax.shard_map(
        shards, mesh=mesh, in_specs=placed, out_specs=P("member", None, "space"), check_vma=False
    )
```

time: 156 us -> 66.8 us (0.43)
  blocking collectives: 65.7 us -> 0 us
  Pallas kernels: 0 us -> 52 us
  matrix products: 44.6 us -> 0 us
  between operations: 16.7 us -> 0.07 us
  starting transfers between devices: 12.1 us -> 0 us
  other arithmetic: 10.5 us -> 0 us
  local copies, waits for them, and re-layouts: 4.16 us -> 14.1 us
    all_gather x5 -> x0, blocking collectives: 65.7 us -> none  [the longest x1 20.8 us: shards(): lax.all_gather(pick_rows(normed, published), 'space', axis=0, tiled=True)]
    pallas_call x0 -> x1, Pallas kernels: none -> 52 us  [shards(): pl.pallas_call(functools.partial(kernel, bands), out_shape=jax.ShapeDtype...]
    dot_general x30 -> x0, matrix products: 44.6 us -> none  [the longest x6 8.68 us: adjacency(): lax.dot_general(dst_hot, src_hot, (((0,), (0,)), ((), ())), preferred_ele...]
    unnamed x56 -> x41, local copies, waits for them, and re-layouts: 0.15 us -> 14.1 us
    ppermute x4 -> x0, starting transfers between devices: 12 us -> none  [from_behind(): return lax.ppermute(block, axis, route)]
    lt x12 -> x0, other arithmetic: 7.69 us -> none  [the longest x8 5.39 us: adjacency(): live_slot = start + lax.broadcasted_iota(jnp.int32, (block, 1), 0) < length]
    dynamic_slice x3 -> x0, local copies, waits for them, and re-layouts: 3.41 us -> none  [the longest x1 1.37 us: shards(): m2g_src[0][lower]]
    reduce_sum x3 -> x0, other arithmetic: 2.03 us -> none  [the longest x1 1.61 us: attend_block(): jnp.sum((label_block[:, :, None] == lax.broadcasted_iota(jnp.int32, (1, 1...]
  transfers between devices with their start and end apart: 6 -> 0, of which waited for: 1 -> 0; matrix products, arithmetic and copies ran while one was open for 31% -> 0% of each run, Pallas kernels for 0% -> 0%
where the time goes in v1:
time: 66.8 us; the launch traced here: 66.1 us
  Pallas kernels  52 us (78%)
  local copies, waits for them, and re-layouts  14.1 us (21%)
    pallas_call x1, Pallas kernels, shards(): pl.pallas_call(functools.partial(kernel, bands), out_shape=jax.ShapeDtype...  52 us
    unnamed x41, local copies, waits for them, and re-layouts  14.1 us

profile of v1, /device:TPU:1, one launch (start us, length us, event | category | flops | bytes accessed | tf_op | source)
XLA Modules:
  0.0 66.1 jit_solution(1404800603683102894)
XLA Ops:
  0.0 0.0 copy-start.17
  0.0 0.0 copy-start
  0.0 0.8 %copy.30.g2m_len = s32[8,1]{1,0:T(8,128)S(1)} copy(s32[8,1]{0,1:T(1,128)} %param.35) | data formatting | bytes 64 | tf_op args[6]
  0.8 0.0 copy-done.17
  0.8 0.1 copy.32.m2g_len
  0.9 0.9 %copy.31.mesh_nbr = s32[256,32]{1,0:T(8,128)S(1)} copy(s32[256,32]{0,1:T(8,128)} %param.36) | data formatting | bytes 65536 | tf_op args[7]
  1.7 0.0 copy-start.2
  1.7 0.0 copy-start.16
  1.7 1.1 %copy.33.w_out = bf16[512,84]{1,0:T(8,128)(2,1)S(1)} copy(bf16[512,84]{0,1:T(8,128)(2,1)} %param.57) | data formatting | bytes 172032 | tf_op args[28]
  2.8 0.0 copy-done
  2.8 0.0 copy-done.2
  2.8 0.0 copy-done.16
  2.8 0.0 copy-start.1
  2.8 0.9 %copy-done.1 = bf16[256,512]{1,0:T(8,128)(2,1)S(1)} copy-done((bf16[256,512]{1,0:T(8,128)(2,1)S(1)}, bf16[256,512]{1,0:T(8,128)(2,1)}, u32[]{:S(2)}) %copy-start.1) | copy-done | bytes 262168
  3.8 0.0 copy-start.3
  3.8 0.9 %copy-done.3 = bf16[128,512]{1,0:T(8,128)(2,1)S(1)} copy-done((bf16[128,512]{1,0:T(8,128)(2,1)S(1)}, bf16[128,512]{1,0:T(8,128)(2,1)}, u32[]{:S(2)}) %copy-start.3) | copy-done | bytes 131096
  4.7 0.0 copy-start.4
  4.7 0.9 %copy-done.4 = bf16[128,512]{1,0:T(8,128)(2,1)S(1)} copy-done((bf16[128,512]{1,0:T(8,128)(2,1)S(1)}, bf16[128,512]{1,0:T(8,128)(2,1)}, u32[]{:S(2)}) %copy-start.4) | copy-done | bytes 131096
  5.6 0.0 copy-start.5
  5.6 0.9 %copy-done.5 = bf16[128,512]{1,0:T(8,128)(2,1)S(1)} copy-done((bf16[128,512]{1,0:T(8,128)(2,1)S(1)}, bf16[128,512]{1,0:T(8,128)(2,1)}, u32[]{:S(2)}) %copy-start.5) | copy-done | bytes 131096
  6.5 0.0 copy-start.6
  6.5 0.7 %copy-done.6 = s32[1,2560]{1,0:T(1,128)S(1)} copy-done((s32[1,2560]{1,0:T(1,128)S(1)}, s32[1,2560]{1,0:T(1,128)}, u32[]{:S(2)}) %copy-start.6) | copy-done | bytes 10264
  7.2 0.0 copy-start.7
  7.2 0.7 %copy-done.7 = s32[1,2560]{1,0:T(1,128)S(1)} copy-done((s32[1,2560]{1,0:T(1,128)S(1)}, s32[1,2560]{1,0:T(1,128)}, u32[]{:S(2)}) %copy-start.7) | copy-done | bytes 10264
  7.9 0.0 copy-start.8
  7.9 0.7 %copy-done.8 = s32[1,8,256]{2,1,0:T(8,128)S(1)} copy-done((s32[1,8,256]{2,1,0:T(8,128)S(1)}, s32[1,8,256]{2,1,0:T(8,128)}, u32[]{:S(2)}) %copy-start.8) | copy-done | bytes 8216
  8.6 0.0 copy-start.9
  8.6 0.7 %copy-done.9 = s32[1,8,256]{2,1,0:T(8,128)S(1)} copy-done((s32[1,8,256]{2,1,0:T(8,128)S(1)}, s32[1,8,256]{2,1,0:T(8,128)}, u32[]{:S(2)}) %copy-start.9) | copy-done | bytes 8216
  9.3 0.0 copy-start.10
  9.3 0.7 %copy-done.10 = s32[1,8,256]{2,1,0:T(8,128)S(1)} copy-done((s32[1,8,256]{2,1,0:T(8,128)S(1)}, s32[1,8,256]{2,1,0:T(8,128)}, u32[]{:S(2)}) %copy-start.10) | copy-done | bytes 8216
  10.0 0.0 copy-start.11
  10.0 0.7 %copy-done.11 = s32[1,8,256]{2,1,0:T(8,128)S(1)} copy-done((s32[1,8,256]{2,1,0:T(8,128)S(1)}, s32[1,8,256]{2,1,0:T(8,128)}, u32[]{:S(2)}) %copy-start.11) | copy-done | bytes 8216
  10.7 0.0 copy-start.12
  10.7 0.7 %copy-done.12 = s32[1,1536]{1,0:T(1,128)S(1)} copy-done((s32[1,1536]{1,0:T(1,128)S(1)}, s32[1,1536]{1,0:T(1,128)}, u32[]{:S(2)}) %copy-start.12) | copy-done | bytes 6168
  11.4 0.0 copy-start.13
  11.4 0.7 %copy-done.13 = s32[1,1536]{1,0:T(1,128)S(1)} copy-done((s32[1,1536]{1,0:T(1,128)S(1)}, s32[1,1536]{1,0:T(1,128)}, u32[]{:S(2)}) %copy-start.13) | copy-done | bytes 6168
  12.1 0.0 copy-start.14
  12.1 0.7 %copy-done.14 = f32[512]{0:T(512)S(1)} copy-done((f32[512]{0:T(512)S(1)}, f32[512]{0:T(512)}, u32[]{:S(2)}) %copy-start.14) | copy-done | bytes 2072
  12.8 0.0 copy-start.15
  12.8 0.7 %copy-done.15 = f32[512]{0:T(512)S(1)} copy-done((f32[512]{0:T(512)S(1)}, f32[512]{0:T(512)}, u32[]{:S(2)}) %copy-start.15) | copy-done | bytes 2072
  13.4 52.0 %shard_map.271 = bf16[84,1024]{1,0:T(8,128)(2,1)S(1)} custom-call(bf16[1,1024,256]{2,1,0:T(8,128)(2,1)} %grid_in.1, bf16[256,512]{1,0:T(8,128)(2,1)S(1)} %copy-done, s32[1,8,256]{2,1,0:T(8,128)S(1)} %copy-done.8, s32[1,8,256]{2,1,0:T(8,128)S(1)} %copy-done.9, s32[1,1536]{1,0:T(1,128)S(1)} %copy-done.12, s32[1,1536]{1,0:T(1,128)S(1)} %copy-done.13, ...), custom_call_target="tpu_custom_call" | custom-call | flops 8000000000 | bytes 6000000 | tf_op jit(solution)/shard_map/pallas_call | solution.py:386
  65.4 0.7 %copy.35 = bf16[1,84,1024]{2,1,0:T(8,128)(2,1)} copy(bf16[1,84,1024]{2,1,0:T(8,128)(2,1)S(1)} %bitcast.1) | data formatting | bytes 344064
Async XLA Ops:
  0.0 0.8 %copy-start.17 = (s32[8,1]{0,1:T(1,128)S(1)}, s32[8,1]{0,1:T(1,128)}, u32[]{:S(2)}) copy-start(s32[8,1]{0,1:T(1,128)} %param.42) | copy-start | bytes 100
  0.0 2.8 %copy-start = (bf16[256,512]{1,0:T(8,128)(2,1)S(1)}, bf16[256,512]{1,0:T(8,128)(2,1)}, u32[]{:S(2)}) copy-start(bf16[256,512]{1,0:T(8,128)(2,1)} %mesh_embed.1) | copy-start | bytes 786436
  1.7 1.1 %copy-start.2 = (bf16[128,512]{1,0:T(8,128)(2,1)S(1)}, bf16[128,512]{1,0:T(8,128)(2,1)}, u32[]{:S(2)}) copy-start(bf16[128,512]{1,0:T(8,128)(2,1)} %w_query.1) | copy-start | bytes 393220
  1.7 1.1 %copy-start.16 = (s32[1,16]{1,0:T(1,128)S(1)}, s32[1,16]{1,0:T(1,128)}, u32[]{:S(2)}) copy-start(s32[1,16]{1,0:T(1,128)} %halo_rows.1) | copy-start | bytes 196
  2.8 1.0 %copy-start.1 = (bf16[256,512]{1,0:T(8,128)(2,1)S(1)}, bf16[256,512]{1,0:T(8,128)(2,1)}, u32[]{:S(2)}) copy-start(bf16[256,512]{1,0:T(8,128)(2,1)} %w_embed.1) | copy-start | bytes 786436
  3.8 0.9 %copy-start.3 = (bf16[128,512]{1,0:T(8,128)(2,1)S(1)}, bf16[128,512]{1,0:T(8,128)(2,1)}, u32[]{:S(2)}) copy-start(bf16[128,512]{1,0:T(8,128)(2,1)} %w_key.1) | copy-start | bytes 393220
  4.7 0.9 %copy-start.4 = (bf16[128,512]{1,0:T(8,128)(2,1)S(1)}, bf16[128,512]{1,0:T(8,128)(2,1)}, u32[]{:S(2)}) copy-start(bf16[128,512]{1,0:T(8,128)(2,1)} %w_value.1) | copy-start | bytes 393220
  5.6 0.9 %copy-start.5 = (bf16[128,512]{1,0:T(8,128)(2,1)S(1)}, bf16[128,512]{1,0:T(8,128)(2,1)}, u32[]{:S(2)}) copy-start(bf16[128,512]{1,0:T(8,128)(2,1)} %w_project.1) | copy-start | bytes 393220
  6.5 0.7 %copy-start.6 = (s32[1,2560]{1,0:T(1,128)S(1)}, s32[1,2560]{1,0:T(1,128)}, u32[]{:S(2)}) copy-start(s32[1,2560]{1,0:T(1,128)} %m2g_own_src.1) | copy-start | bytes 30724
  7.2 0.7 %copy-start.7 = (s32[1,2560]{1,0:T(1,128)S(1)}, s32[1,2560]{1,0:T(1,128)}, u32[]{:S(2)}) copy-start(s32[1,2560]{1,0:T(1,128)} %m2g_own_dst.1) | copy-start | bytes 30724
  7.9 0.7 %copy-start.8 = (s32[1,8,256]{2,1,0:T(8,128)S(1)}, s32[1,8,256]{2,1,0:T(8,128)}, u32[]{:S(2)}) copy-start(s32[1,8,256]{2,1,0:T(8,128)} %g2m_src.1) | copy-start | bytes 24580
  8.6 0.7 %copy-start.9 = (s32[1,8,256]{2,1,0:T(8,128)S(1)}, s32[1,8,256]{2,1,0:T(8,128)}, u32[]{:S(2)}) copy-start(s32[1,8,256]{2,1,0:T(8,128)} %g2m_dst.1) | copy-start | bytes 24580
  9.3 0.7 %copy-start.10 = (s32[1,8,256]{2,1,0:T(8,128)S(1)}, s32[1,8,256]{2,1,0:T(8,128)}, u32[]{:S(2)}) copy-start(s32[1,8,256]{2,1,0:T(8,128)} %m2g_src.1) | copy-start | bytes 24580
  10.0 0.7 %copy-start.11 = (s32[1,8,256]{2,1,0:T(8,128)S(1)}, s32[1,8,256]{2,1,0:T(8,128)}, u32[]{:S(2)}) copy-start(s32[1,8,256]{2,1,0:T(8,128)} %m2g_dst.1) | copy-start | bytes 24580
  10.7 0.7 %copy-start.12 = (s32[1,1536]{1,0:T(1,128)S(1)}, s32[1,1536]{1,0:T(1,128)}, u32[]{:S(2)}) copy-start(s32[1,1536]{1,0:T(1,128)} %g2m_own_src.1) | copy-start | bytes 18436
  11.4 0.7 %copy-start.13 = (s32[1,1536]{1,0:T(1,128)S(1)}, s32[1,1536]{1,0:T(1,128)}, u32[]{:S(2)}) copy-start(s32[1,1536]{1,0:T(1,128)} %g2m_own_dst.1) | copy-start | bytes 18436
  12.1 0.7 %copy-start.14 = (f32[512]{0:T(512)S(1)}, f32[512]{0:T(512)}, u32[]{:S(2)}) copy-start(f32[512]{0:T(512)} %attn_gain.1) | copy-start | bytes 6148
  12.8 0.7 %copy-start.15 = (f32[512]{0:T(512)S(1)}, f32[512]{0:T(512)}, u32[]{:S(2)}) copy-start(f32[512]{0:T(512)} %mlp_gain.1) | copy-start | bytes 6148

commit v2 on v1

--- a/solution.py
+++ b/solution.py
@@ -56,14 +56,23 @@
     return jnp.where(iota(row.shape, 1) + start < length, row, -1)
 
 
-def kernel(
-    bands, grid_in, mesh_embed, g2m_src, g2m_dst, g2m_own_src, g2m_own_dst, g2m_len, mesh_nbr,
-    halo_rows, m2g_src, m2g_dst, m2g_own_src, m2g_own_dst, m2g_len, w_embed, w_send, w_mesh,
-    attn_gain, w_query, w_key, w_value, w_project, mlp_gain, w_up, w_down, w_return, w_grid,
-    w_skip, w_out, out, attn_w, up_w, down_w, latent, sends, links, links_acc, back, back_acc,
-    skip, pick_up, pick_dn, from_lo, from_hi, ret_up, ret_dn, back_lo, back_hi, far,
-    wsend, wrecv, msend, mrecv, hsend, hrecv,
-):
+def kernel(bands, *refs):
+    hbm = dict(zip(NAMES, refs))
+    head = refs[len(NAMES) - 1]
+    out = refs[len(NAMES)]
+    rest = refs[len(NAMES) + 1 :]
+    stage = dict(zip(STAGED, rest))
+    (
+        attn_w, up_w, down_w, latent, sends, links, links_acc, back, back_acc,
+        skip, pick_up, pick_dn, from_lo, from_hi, ret_up, ret_dn, back_lo, back_hi, far,
+        expanded, wsend, wrecv, msend, mrecv, hsend, hrecv, fetched,
+    ) = rest[len(STAGED) :]
+    grid_in, mesh_embed, g2m_src, g2m_dst = (stage[n] for n in STAGED[:4])
+    g2m_own_src, g2m_own_dst, g2m_len, mesh_nbr = (stage[n] for n in STAGED[4:8])
+    halo_rows, m2g_src, m2g_dst, m2g_own_src = (stage[n] for n in STAGED[8:12])
+    m2g_own_dst, m2g_len, w_embed, w_send = (stage[n] for n in STAGED[12:16])
+    w_mesh, attn_gain, mlp_gain, w_return = (stage[n] for n in STAGED[16:20])
+    w_grid, w_skip = (stage[n] for n in STAGED[20:])
     me = lax.axis_index("member")
     band = lax.axis_index("space")
     xm = me + 1 - 2 * lax.rem(me, 2)
@@ -86,11 +95,23 @@
         pl.semaphore_signal(
             barrier, inc=1, device_id=(me, lax.rem(band + off, bands)), device_id_type=MESH
         )
-    for i, ref in enumerate((w_query, w_key, w_value, w_project)):
-        attn_w[me, i] = ref[...]
-    up_w[me] = w_up[...]
-    down_w[me] = w_down[...]
+    homes = {
+        "w_query": attn_w.at[me, 0], "w_key": attn_w.at[me, 1], "w_value": attn_w.at[me, 2],
+        "w_project": attn_w.at[me, 3], "w_up": up_w.at[me], "w_down": down_w.at[me],
+    }
+
+    def fetch(name):
+        target = homes[name] if name in homes else stage[name]
+        return pltpu.make_async_copy(hbm[name], target, fetched.at[NAMES.index(name)])
+
+    def ready(*names):
+        for name in names:
+            fetch(name).wait()
+
+    for name in FETCH_ORDER:
+        fetch(name).start()
     pl.semaphore_wait(barrier, bands + 1)
+    ready("w_query", "w_key", "w_value", "w_project")
 
     def piece(group, slot, part):
         def rows(total):
@@ -138,6 +159,8 @@
 
     wstart(0, "ab")
 
+    ready("grid_in", "w_embed", "w_send", "g2m_src")
+
     block = 256
 
     def embed(i, carry):
@@ -161,10 +184,14 @@
 
     wwait(0, "ab")
     wstart(0, "cdef")
+    ready("w_up", "w_down")
     wstart(1, "ab")
+    ready("g2m_len", "g2m_own_src", "g2m_own_dst", "g2m_dst", "w_mesh", "mesh_embed")
+    ready("attn_gain", "halo_rows", "mesh_nbr", "m2g_len", "m2g_own_src", "m2g_own_dst")
+    ready("mlp_gain", "m2g_src", "m2g_dst", "w_skip", "w_return", "w_grid")
 
     links_acc[...] = jnp.zeros_like(links_acc)
-    own_length = g2m_len[band, 0]
+    own_length = g2m_len[0, band]
 
     def own_links(i, carry):
         start = pl.multiple_of(i * EDGE_BLOCK, EDGE_BLOCK)
@@ -179,9 +206,6 @@
 
     wwait(0, "cd")
     wstart(0, "g")
-    wwait(1, "ab")
-    wstart(1, "cdef")
-    wstart(2, "ab")
 
     @pl.when(has_lower)
     def _():
@@ -199,14 +223,14 @@
     def _():
         from_hi[...] = jnp.zeros_like(from_hi)
 
-    len_lo = jnp.where(has_lower, g2m_len[lower, 0], 0)
-    len_hi = jnp.where(has_upper, g2m_len[upper, 0], 0)
+    len_lo = jnp.where(has_lower, g2m_len[0, lower], 0)
+    len_hi = jnp.where(has_upper, g2m_len[0, upper], 0)
     place_lo = one_hot_t(live(g2m_dst[0, pl.ds(lower, 1), :], len_lo), mesh_rows)
     place_hi = one_hot_t(live(g2m_dst[0, pl.ds(upper, 1), :], len_hi), mesh_rows)
     mesh_agg = mesh_agg + dot(place_lo, from_lo[...]) + dot(place_hi, from_hi[...])
     update = silu(dot(mesh_agg.astype(BF), w_mesh[...]))
     mesh_state = (mesh_embed[...].astype(F32) + update).astype(BF)
-    normed = layer_norm(mesh_state.astype(F32), attn_gain[...].reshape(1, width)).astype(BF)
+    normed = layer_norm(mesh_state.astype(F32), attn_gain[...]).astype(BF)
 
     wanted = jnp.zeros((hb, mesh_rows), jnp.int32)
     for j in range(hb):
@@ -232,12 +256,16 @@
     for off in range(1, bands):
         halo(off).start()
 
+    wwait(1, "ab")
+    wstart(1, "cdef")
+    wstart(2, "ab")
+
     table = mesh_rows + bands * hb
-    nbr = mesh_nbr[...]
-    label = iota((mesh_rows, table), 1)
-    repeats = jnp.where(label == iota((mesh_rows, table), 0), 1.0, 0.0)
-    for k in range(nbr.shape[1]):
-        repeats = repeats + jnp.where(nbr[:, k : k + 1] == label, 1.0, 0.0)
+    label = iota((table, mesh_rows), 0)
+    repeats = jnp.where(label == iota((table, mesh_rows), 1), 1.0, 0.0)
+    for k in range(mesh_nbr.shape[0]):
+        repeats = repeats + jnp.where(mesh_nbr[k : k + 1, :] == label, 1.0, 0.0)
+    repeats = jnp.transpose(repeats)
 
     wwait(0, "efg")
 
@@ -247,11 +275,6 @@
     queries = dot(normed, attn_full(0)).astype(BF)
     key_local = dot(normed, attn_full(1)).astype(BF)
     value_local = dot(normed, attn_full(2)).astype(BF)
-
-    wwait(1, "cd")
-    wstart(1, "g")
-    wwait(2, "ab")
-    wstart(2, "cdef")
 
     for off in range(1, bands):
         halo_in(off).wait_recv()
@@ -268,13 +291,15 @@
         mixed.append(dot(probs, values[:, cols]).astype(BF))
     attended = jnp.concatenate(mixed, axis=1)
     after_attn = mesh_state.astype(F32) + dot(attended, attn_full(3))
-    normed_two = layer_norm(after_attn, mlp_gain[...].reshape(1, width)).astype(BF)
-
-    wwait(2, "cd")
-    wstart(2, "g")
+    normed_two = layer_norm(after_attn, mlp_gain[...]).astype(BF)
+
+    wwait(1, "cd")
+    wstart(1, "g")
+    wwait(2, "ab")
+    wstart(2, "cdef")
 
     back_acc[...] = jnp.zeros_like(back_acc)
-    back_length = m2g_len[band, 0]
+    back_length = m2g_len[0, band]
 
     def own_back(i, carry):
         start = pl.multiple_of(i * EDGE_BLOCK, EDGE_BLOCK)
@@ -286,67 +311,63 @@
     lax.fori_loop(0, m2g_own_src.shape[1] // EDGE_BLOCK, own_back, 0)
     back[...] = back_acc[...].astype(BF)
 
+    wwait(2, "cd")
+    wstart(2, "g")
+
+    wwait(1, "efg")
+    hidden = down_w.shape[1]
+    for j in range(down_w.shape[0]):
+        up = up_w[:, :, j * hidden : (j + 1) * hidden].reshape(width, hidden)
+        expanded[j] = silu(dot(normed_two, up)).astype(BF)
+    total = after_attn + dot(expanded[me], down_w[me])
+    for kind, slot in (("e", xm), ("f", ym), ("g", dm)):
+        wwait(2, kind)
+        total = total + dot(expanded[slot], down_w[slot])
+    mesh_out = total.astype(BF)
+    return_rows = dot(mesh_out, w_return[...]).astype(BF)
+    ret_up[...] = dot(one_hot(m2g_src[0, pl.ds(upper, 1), :], mesh_rows), return_rows).astype(BF)
+    ret_dn[...] = dot(one_hot(m2g_src[0, pl.ds(lower, 1), :], mesh_rows), return_rows).astype(BF)
+
+    @pl.when(has_upper)
+    def _():
+        message(2, ret_up, back_lo, upper).start()
+
+    @pl.when(has_lower)
+    def _():
+        message(3, ret_dn, back_hi, lower).start()
+
     def skip_rows(i, carry):
         rows = pl.ds(pl.multiple_of(i * block, block), block)
         skip[rows, :] = dot(latent[rows, :], w_skip[...])
         return carry
 
     lax.fori_loop(0, grid_rows // block, skip_rows, 0)
-
-    wwait(1, "efg")
-    hidden = down_w.shape[1]
-    expanded = []
-    for j in range(down_w.shape[0]):
-        up = up_w[:, :, j * hidden : (j + 1) * hidden].reshape(width, hidden)
-        expanded.append(silu(dot(normed_two, up)).astype(BF))
-    wwait(2, "efg")
-    total = after_attn
-    for j in range(down_w.shape[0]):
-        total = total + dot(expanded[j], down_w[j])
-    mesh_out = total.astype(BF)
-    return_rows = dot(mesh_out, w_return[...]).astype(BF)
-    ret_up[...] = dot(one_hot(m2g_src[0, pl.ds(upper, 1), :], mesh_rows), return_rows).astype(BF)
-    ret_dn[...] = dot(one_hot(m2g_src[0, pl.ds(lower, 1), :], mesh_rows), return_rows).astype(BF)
-
-    @pl.when(has_upper)
-    def _():
-        message(2, ret_up, back_lo, upper).start()
-
-    @pl.when(has_lower)
-    def _():
-        message(3, ret_dn, back_hi, lower).start()
-
     agg = dot(back[...], return_rows)
-
-    @pl.when(has_lower)
-    def _():
-        message(2, ret_up, back_lo, upper).wait_recv()
-
-    @pl.when(has_upper)
-    def _():
-        message(3, ret_dn, back_hi, lower).wait_recv()
-
-    @pl.when(jnp.logical_not(has_lower))
-    def _():
-        back_lo[...] = jnp.zeros_like(back_lo)
-
-    @pl.when(jnp.logical_not(has_upper))
-    def _():
-        back_hi[...] = jnp.zeros_like(back_hi)
-
-    blen_lo = jnp.where(has_lower, m2g_len[lower, 0], 0)
-    blen_hi = jnp.where(has_upper, m2g_len[upper, 0], 0)
+    blen_lo = jnp.where(has_lower, m2g_len[0, lower], 0)
+    blen_hi = jnp.where(has_upper, m2g_len[0, upper], 0)
     land_lo = one_hot_t(live(m2g_dst[0, pl.ds(lower, 1), :], blen_lo), grid_rows)
     land_hi = one_hot_t(live(m2g_dst[0, pl.ds(upper, 1), :], blen_hi), grid_rows)
+
+    @pl.when(has_lower)
+    def _():
+        message(2, ret_up, back_lo, upper).wait_recv()
+
+    @pl.when(has_upper)
+    def _():
+        message(3, ret_dn, back_hi, lower).wait_recv()
+
+    @pl.when(jnp.logical_not(has_lower))
+    def _():
+        back_lo[...] = jnp.zeros_like(back_lo)
+
+    @pl.when(jnp.logical_not(has_upper))
+    def _():
+        back_hi[...] = jnp.zeros_like(back_hi)
+
     agg = agg + dot(land_lo, back_lo[...]) + dot(land_hi, back_hi[...])
     pre = dot(agg.astype(BF), w_grid[...]) + skip[...]
     updated = silu(pre).astype(BF)
-    f_out = w_out.shape[1]
-    padded = jnp.concatenate(
-        [w_out[...].astype(F32), jnp.zeros((width, 128 - f_out), F32)], axis=1
-    )
-    head = jnp.transpose(padded).astype(BF)
-    out[...] = dot_nt(head, updated)[:f_out].astype(BF)
+    out[...] = dot_nt(head[...], updated).astype(BF)
 
     for group in range(3):
         for kind in "abcdefg":
@@ -365,10 +386,29 @@
         message(3, ret_dn, back_hi, lower).wait_send()
 
 
-SCALAR_ARGS = (6, 8, 13)
+NAMES = (
+    "grid_in", "mesh_embed", "g2m_src", "g2m_dst", "g2m_own_src", "g2m_own_dst", "g2m_len",
+    "mesh_nbr", "halo_rows", "m2g_src", "m2g_dst", "m2g_own_src", "m2g_own_dst", "m2g_len",
+    "w_embed", "w_send", "w_mesh", "attn_gain", "w_query", "w_key", "w_value", "w_project",
+    "mlp_gain", "w_up", "w_down", "w_return", "w_grid", "w_skip", "w_out",
+)
+SHARDED = ("w_query", "w_key", "w_value", "w_project", "w_up", "w_down")
+STAGED = tuple(n for n in NAMES[:-1] if n not in SHARDED)
+SCALARS = ("g2m_len", "halo_rows", "m2g_len")
+FIRST = ("w_query", "w_key", "w_value", "w_project", "grid_in", "w_embed", "w_send", "g2m_src")
+FETCH_ORDER = FIRST + ("w_up", "w_down") + tuple(
+    n for n in STAGED if n not in FIRST
+)
 
 
 def shards(*args):
+    args = list(args)
+    for name in ("g2m_len", "m2g_len", "mesh_nbr", "w_out"):
+        i = NAMES.index(name)
+        args[i] = args[i].T
+    for name in ("attn_gain", "mlp_gain"):
+        i = NAMES.index(name)
+        args[i] = args[i].reshape(1, -1)
     grid_rows = args[0].shape[1]
     mesh_rows, width = args[1].shape
     slots = args[2].shape[2]
@@ -377,18 +417,21 @@
     members = lax.axis_size("member")
     depth, ffn = args[23].shape
     down = args[24].shape
-    f_out = args[28].shape[1]
+    f_out = args[28].shape[0]
+    named = dict(zip(NAMES, args))
+    staging = [
+        (pltpu.SMEM if n in SCALARS else pltpu.VMEM)(named[n].shape, named[n].dtype)
+        for n in STAGED
+    ]
     msg = pltpu.VMEM((slots, width), BF)
-    in_specs = [
-        pl.BlockSpec(memory_space=pltpu.SMEM if i in SCALAR_ARGS else pltpu.VMEM)
-        for i in range(len(args))
-    ]
+    in_specs = [pl.BlockSpec(memory_space=pltpu.HBM)] * (len(args) - 1)
+    in_specs.append(pl.BlockSpec(memory_space=pltpu.VMEM))
     result = pl.pallas_call(
         functools.partial(kernel, bands),
         out_shape=jax.ShapeDtypeStruct((f_out, grid_rows), BF),
         in_specs=in_specs,
         out_specs=pl.BlockSpec(memory_space=pltpu.VMEM),
-        scratch_shapes=[
+        scratch_shapes=staging + [
             pltpu.VMEM((members, 4, depth, width), BF),
             pltpu.VMEM((members, depth, ffn), BF),
             pltpu.VMEM((members,) + tuple(down), BF),
@@ -401,15 +444,17 @@
             pltpu.VMEM((grid_rows, width), F32),
             msg, msg, msg, msg, msg, msg, msg, msg,
             pltpu.VMEM((bands * hb, width), BF),
+            pltpu.VMEM((members, mesh_rows, down[0]), BF),
             pltpu.SemaphoreType.DMA((3, 7)),
             pltpu.SemaphoreType.DMA((3, 7)),
             pltpu.SemaphoreType.DMA((4,)),
             pltpu.SemaphoreType.DMA((4,)),
             pltpu.SemaphoreType.DMA((bands,)),
             pltpu.SemaphoreType.DMA((bands,)),
+            pltpu.SemaphoreType.DMA((len(NAMES),)),
         ],
         compiler_params=pltpu.CompilerParams(
-            collective_id=0, has_side_effects=True, vmem_limit_bytes=52 * 1024 * 1024
+            collective_id=0, has_side_effects=True, vmem_limit_bytes=66060288
         ),
         cost_estimate=pl.CostEstimate(
             flops=8_000_000_000, bytes_accessed=6_000_000, transcendentals=3_000_000

time: 66.8 us -> 49.7 us (0.74)
  local copies, waits for them, and re-layouts: 14.1 us -> 1.61 us
  Pallas kernels: 52 us -> 47.9 us
    unnamed x41 -> x1, local copies, waits for them, and re-layouts: 14.1 us -> 1.61 us
    pallas_call x1, Pallas kernels: 52 us -> 47.9 us  [shards(): pl.pallas_call(functools.partial(kernel, bands), out_shape=jax.ShapeDtype...]
where the time goes in v2:
time: 49.7 us; the launch traced here: 49.5 us
  Pallas kernels  47.9 us (96%)
  local copies, waits for them, and re-layouts  1.61 us (3%)
    pallas_call x1, Pallas kernels, shards(): pl.pallas_call(functools.partial(kernel, bands), out_shape=jax.ShapeDtype...  47.9 us
    unnamed x1, local copies, waits for them, and re-layouts  1.61 us

profile of v2, /device:TPU:1, one launch (start us, length us, event | category | flops | bytes accessed | tf_op | source)
XLA Modules:
  0.0 49.5 jit_solution(4963138673577312812)
XLA Ops:
  0.0 47.9 %shard_map.271 = bf16[84,1024]{1,0:T(8,128)(2,1)} custom-call(bf16[1,1024,256]{2,1,0:T(8,128)(2,1)} %refs_0_.1, bf16[256,512]{1,0:T(8,128)(2,1)} %refs_1_.1, s32[1,8,256]{2,1,0:T(8,128)} %refs_2_.1, s32[1,8,256]{2,1,0:T(8,128)} %refs_3_.1, s32[1,1536]{1,0:T(1,128)} %refs_4_.1, s32[1,1536]{1,0:T(1,128)} %refs_5_.1, s32[1,8]{1,0:T(1,128)} %bitcast.12, ...), custom_call_target="tpu_custom_call" | custom-call | flops 8000000000 | bytes 6000000 | tf_op jit(solution)/shard_map/pallas_call | solution.py:429
  47.9 1.6 %copy.31 = bf16[1,84,1024]{2,1,0:T(8,128)(2,1)} copy(bf16[1,84,1024]{2,1,0:T(8,128)(2,1)} %bitcast.7) | data formatting | bytes 344064

commit v3 on v2

--- a/solution.py
+++ b/solution.py
@@ -158,6 +158,8 @@
         )
 
     wstart(0, "ab")
+    ready("w_up", "w_down")
+    wstart(1, "ab")
 
     ready("grid_in", "w_embed", "w_send", "g2m_src")
 
@@ -184,8 +186,7 @@
 
     wwait(0, "ab")
     wstart(0, "cdef")
-    ready("w_up", "w_down")
-    wstart(1, "ab")
+    wstart(2, "ab")
     ready("g2m_len", "g2m_own_src", "g2m_own_dst", "g2m_dst", "w_mesh", "mesh_embed")
     ready("attn_gain", "halo_rows", "mesh_nbr", "m2g_len", "m2g_own_src", "m2g_own_dst")
     ready("mlp_gain", "m2g_src", "m2g_dst", "w_skip", "w_return", "w_grid")
@@ -258,7 +259,6 @@
 
     wwait(1, "ab")
     wstart(1, "cdef")
-    wstart(2, "ab")
 
     table = mesh_rows + bands * hb
     label = iota((table, mesh_rows), 0)

time: 49.7 us -> 47.5 us (0.956)
  Pallas kernels: 47.9 us -> 45.7 us
    pallas_call x1, Pallas kernels: 47.9 us -> 45.7 us  [shards(): pl.pallas_call(functools.partial(kernel, bands), out_shape=jax.ShapeDtype...]
where the time goes in v3:
time: 47.5 us; the launch traced here: 47.3 us
  Pallas kernels  45.7 us (96%)
  local copies, waits for them, and re-layouts  1.61 us (3%)
    pallas_call x1, Pallas kernels, shards(): pl.pallas_call(functools.partial(kernel, bands), out_shape=jax.ShapeDtype...  45.7 us
    unnamed x1, local copies, waits for them, and re-layouts  1.61 us

profile of v3, /device:TPU:1, one launch (start us, length us, event | category | flops | bytes accessed | tf_op | source)
XLA Modules:
  0.0 47.3 jit_solution(3708082504105937577)
XLA Ops:
  0.0 45.7 %shard_map.271 = bf16[84,1024]{1,0:T(8,128)(2,1)} custom-call(bf16[1,1024,256]{2,1,0:T(8,128)(2,1)} %refs_0_.1, bf16[256,512]{1,0:T(8,128)(2,1)} %refs_1_.1, s32[1,8,256]{2,1,0:T(8,128)} %refs_2_.1, s32[1,8,256]{2,1,0:T(8,128)} %refs_3_.1, s32[1,1536]{1,0:T(1,128)} %refs_4_.1, s32[1,1536]{1,0:T(1,128)} %refs_5_.1, s32[1,8]{1,0:T(1,128)} %bitcast.12, ...), custom_call_target="tpu_custom_call" | custom-call | flops 8000000000 | bytes 6000000 | tf_op jit(solution)/shard_map/pallas_call | solution.py:429
  45.7 1.6 %copy.31 = bf16[1,84,1024]{2,1,0:T(8,128)(2,1)} copy(bf16[1,84,1024]{2,1,0:T(8,128)(2,1)} %bitcast.7) | data formatting | bytes 344064
